TPU v7x, 512 devices: a whole 4x4x16 slice. The times are simulated.
512 devices in a mesh: frames: 64 (over z, y_hi, core), mp: 4 (over x), dp: 2 (over y_lo).
Axes of the slice: x: 4, y: 4 (y_hi: 2, y_lo: 2; y = y_hi * 2 + y_lo), z: 16, core: 2. Of those that a mesh axis runs over, the one named last changes fastest.
Arguments:
- projections: bfloat16 [2, 128, 96, 3, 3584], P('dp', 'frames', None, None, 'mp'), may hold values from -18 to 18
- perturbation: bfloat16 [2, 128, 96, 3, 3584], P('dp', 'frames', None, None, 'mp'), may hold values from -44 to 44
- out_weight: bfloat16 [3584, 3584], P('frames', 'mp'), may hold values from -0.09375 to 0.09375
- norm_gain: float32 [3584], P('mp'), may hold values from 0.25 to 1.75
- live_counts: int32 [2, 128], P('dp'), may hold values from 72 to 96, as said below
Outputs:
- features: bfloat16 [2, 128, 96, 3584], P('dp', 'frames', None, 'mp')
- penalty: float32 [2], P('dp')
- gain_grad: float32 [3584], P('mp')
Inputs may be any that keep to these rules, and one draw needn't show every extreme that they name: `live_counts`: in each clip one slot has all 96 tokens live and another has 72 live.
All inputs are finite; a program needn't handle non-finite values.
Results may differ from a plain program's by a relative error of at most 0.0057.
Values may be sent and summed in bfloat16 or wider, within the bound.
A program may use at most 64 MiB of HBM per device.

v0:
```python
import math
import jax
import jax.numpy as jnp
from jax import lax
from jax.sharding import PartitionSpec as P

HEAD_DIM = 128
sigma_noise = 0.25
epsilon = 1e-06


def padded(cells, sides, width):
    for axis, dim in sides:
        count = lax.axis_size(axis)
        ends = count - 1
        head = lax.slice_in_dim(cells, 0, width, axis=dim)
        tail = lax.slice_in_dim(cells, cells.shape[dim] - width, cells.shape[dim], axis=dim)
        cells = jnp.concatenate(
            [
                lax.ppermute(tail, axis, [(i, (i + 1) % count) for i in range(ends)]),
                cells,
                lax.ppermute(head, axis, [((i + 1) % count, i) for i in range(ends)]),
            ],
            axis=dim,
        )
    return cells


def split_heads(tensor):
    return tensor.reshape(tensor.shape[:-1] + (tensor.shape[-1] // HEAD_DIM, HEAD_DIM))


def attend(query_rows, key_rows, value_rows, key_live):
    scores = jnp.einsum(
        "wrhe,wmhe->whrm",
        split_heads(query_rows),
        split_heads(key_rows),
        preferred_element_type=jnp.float32,
    ) * (1.0 / math.sqrt(HEAD_DIM))
    live_float = key_live[:, None, None, :]
    masked = jnp.where(live_float, scores, -1e30)
    largest = jnp.max(masked, axis=-1, keepdims=True)
    weights = jnp.exp(masked - largest) * live_float.astype(jnp.float32)
    probabilities = (weights / jnp.sum(weights, axis=-1, keepdims=True)).astype(jnp.bfloat16)
    mixed = jnp.einsum(
        "whrm,wmhe->wrhe",
        probabilities,
        split_heads(value_rows),
        preferred_element_type=jnp.float32,
    )
    return mixed.astype(jnp.bfloat16).reshape(query_rows.shape)


def attend_each(query_rows, key_rows, value_rows, key_live):

    def one_window(item):
        return attend(item[0][None], item[1][None], item[2][None], item[3][None])[0]

    return lax.map(one_window, (query_rows, key_rows, value_rows, key_live))


def local(projections, perturbation, out_weight, norm_gain, live_counts):
    tile_len = projections.shape[2]
    local_width = projections.shape[4]
    slab_count = lax.axis_size("frames")
    slab_index = lax.axis_index("frames")
    model_width = local_width * lax.axis_size("mp")
    token_total = projections.shape[1] * slab_count * tile_len
    perturbed = (
        projections.astype(jnp.float32) + sigma_noise * perturbation.astype(jnp.float32)
    ).astype(jnp.bfloat16)
    streams = jnp.concatenate([projections, perturbed], axis=0)
    padded_counts = jnp.pad(live_counts[0], (1, 1))
    nearby = lax.dynamic_slice_in_dim(padded_counts, 2 * slab_index, 4)
    token_pos = jnp.arange(tile_len)
    live_near = token_pos[None, :] < nearby[:, None]
    key_values = streams[:, :, :, 1:, :]
    widened = padded(key_values, (("frames", 1),), 1)
    grouped = widened.reshape(4, 2 * tile_len, 2, local_width)
    query_rows = streams[:, :, :, 0, :].reshape(4, tile_len, local_width)
    key_live = jnp.tile(live_near.reshape(2, 2 * tile_len), (2, 1))
    attended = attend_each(query_rows, grouped[:, :, 0], grouped[:, :, 1], key_live)
    attended = attended.reshape(2, 2, tile_len, local_width)
    gathered = lax.all_gather(attended, "mp", axis=3, tiled=True)
    flat_rows = gathered.reshape(-1, model_width)
    projected = jnp.dot(
        flat_rows,
        lax.all_gather(out_weight, "frames", axis=0, tiled=True),
        preferred_element_type=jnp.float32,
    )
    projected = projected.reshape(2, 2, tile_len, local_width)
    squares = lax.psum(jnp.sum(projected * projected, axis=-1), "mp")
    normed = projected * lax.rsqrt(squares / model_width + epsilon)[..., None]
    own_live = live_near[1:3].astype(jnp.float32)[:, :, None]
    features = (normed[0] * norm_gain * own_live).astype(jnp.bfloat16)[None]
    difference = (normed[1] - normed[0]) * own_live
    feature_sums = jnp.sum(difference * difference, axis=(0, 1))
    local_penalty = jnp.sum(feature_sums * norm_gain * norm_gain).reshape(1)
    penalty = lax.psum(local_penalty, ("frames", "mp")) / (
        sigma_noise * sigma_noise * token_total * model_width
    )
    gain_grad = (
        norm_gain
        * lax.psum(feature_sums, ("frames", "dp"))
        / (sigma_noise * sigma_noise * token_total)
    )
    return (features, penalty, gain_grad)


def solution(mesh):
    placed = (
        P("dp", "frames", None, None, "mp"),
        P("dp", "frames", None, None, "mp"),
        P("frames", "mp"),
        P("mp"),
        P("dp", None),
    )
    return jax.shard_map(
        local,
        mesh=mesh,
        in_specs=placed,
        out_specs=(P("dp", "frames", None, "mp"), P("dp"), P("mp")),
        check_vma=False,
    )
```

profile of v0, /device:TPU:2, one launch (start us, length us, event | category | flops | bytes accessed | tf_op | source)
XLA Modules:
  0.0 1192.0 jit_solution(10483000948008665854)
XLA Ops:
  7.2 0.0 copy-start
  7.2 0.0 all-gather.3.cloned.1.call-start
  7.2 1.9 add_convert_fusion
  9.1 0.0 copy-done
  9.2 0.0 copy-start.2
  9.2 1.2 fusion.25
  10.4 2.6 collective-permute-start
  13.0 1.3 collective-permute-start.1
  14.3 0.0 copy-done.2
  14.3 0.1 pad_dynamic-slice_fusion
  14.4 0.1 lt.41
  14.5 0.1 lt.42
  14.5 0.1 lt.43
  14.6 0.1 lt.38
  14.7 0.1 pad_maximum_fusion.1
  14.8 0.1 fusion.23
  15.0 0.0 collective-permute-done
  15.0 4.5 collective-permute-done.1
  19.5 1.7 pad_maximum_fusion
  21.2 0.3 copy.13
  21.5 1.3 slice_bitcast_fusion
  22.8 22.9 %while.10 = (s32[]{:T(128)}, bf16[4,96,896]{2,1,0:T(8,128)(2,1)}, bf16[4,192,896]{2,1,0:T(8,128)(2,1)}, pred[4,192]{1,0:T(4,128)(4,1)S(1)}, bf16[4,96,896]{2,1,0...) while((s32[]{:T(128)}, bf16[4,96,896]{2,1,0:T(8,128)(2,1)}, bf16[4,192,896]{2,1,0:T(8,128)(2,1)}, ...), condition=%wide.region_3.4_spmd, body=%wide.region_0.3_spmd.sunk | while | flops 67049856 | bytes 5857369 | solution.py:59
  22.8 1.0 constant_dynamic-slice_fusion.5
  23.8 0.4 reshape.106
  24.3 0.2 reshape.107
  24.5 1.5 fusion.45
  26.0 0.4 reshape.108
  26.4 1.4 fusion.46
  27.8 0.7 bitcast_dynamic-update-slice_fusion.2
  28.5 1.0 constant_dynamic-slice_fusion.5
  29.5 0.4 reshape.106
  30.0 0.2 reshape.107
  30.2 1.5 fusion.45
  31.7 0.4 reshape.108
  32.1 1.4 fusion.46
  33.5 0.7 bitcast_dynamic-update-slice_fusion.2
  34.2 1.0 constant_dynamic-slice_fusion.5
  35.3 0.4 reshape.106
  35.7 0.2 reshape.107
  36.0 1.5 fusion.45
  37.5 0.4 reshape.108
  37.9 1.4 fusion.46
  39.3 0.7 bitcast_dynamic-update-slice_fusion.2
  40.0 1.0 constant_dynamic-slice_fusion.5
  41.0 0.4 reshape.106
  41.5 0.2 reshape.107
  41.7 1.5 fusion.45
  43.2 0.4 reshape.108
  43.6 1.4 fusion.46
  45.0 0.7 bitcast_dynamic-update-slice_fusion.2
  45.7 0.0 all-gather.3.cloned.1.call-update
  45.7 0.0 all-gather.5.cloned.1.call-start
  45.8 0.7 all-gather.5.cloned.1.call-update
  46.5 0.1 iota_compare_fusion
  46.5 59.2 %all-gather.3.cloned.1.call-done = bf16[2,2,96,3584]{3,2,1,0:T(8,128)(2,1)} async-done(((bf16[2,2,96,896]{3,2,1,0:T(8,128)(2,1)}), bf16[2,2,96,3584]{3,2,1,0:T(8,128)(2,1)}) %all-gather.3.cloned.1.call-update) | async-done | bytes 2752528 | tf_op jit(solution)/shard_map/all_gather | solution.py:84
  105.8 162.8 %all-gather.5.cloned.1.call-done = bf16[3584,896]{1,0:T(8,128)(2,1)} async-done(((bf16[56,896]{1,0:T(8,128)(2,1)}), bf16[3584,896]{1,0:T(8,128)(2,1)}) %all-gather.5.cloned.1.call-update) | async-done | bytes 6422544 | tf_op jit(solution)/shard_map/all_gather | solution.py:88
  268.6 6.7 multiply_reduce_fusion
  275.3 8.6 psum.21
  283.9 0.2 broadcast_multiply_fusion
  284.1 0.2 fusion.29
  284.3 247.6 %psum.23 = f32[896]{0:T(1024)S(1)} all-reduce(f32[896]{0:T(1024)S(1)} %fusion.29), channel_id=1, replica_groups=mesh['frames'=64,'mp'=4,'dp'=2] {'frames','dp'}, use_global_device_ids=true, to_apply=%region_9.10 | all-reduce | flops 896 | bytes 7168 | tf_op jit(solution)/shard_map/psum | solution.py:104
  532.0 0.8 multiply_convert_fusion
  532.8 1.2 multiply_multiply_fusion.1
  534.0 649.4 %psum.22 = f32[1]{0:T(128)} all-reduce(f32[1]{0:T(128)} %bitcast.11), channel_id=1, replica_groups=mesh['frames'=64,'mp'=4,'dp'=2] {'frames','mp'}, use_global_device_ids=true, to_apply=%region_8.9 | all-reduce | flops 1 | bytes 8 | tf_op jit(solution)/shard_map/psum | solution.py:99
  (21 shorter events, 0.3 us)
Async XLA Ops:
  7.2 2.0 copy-start
  7.2 98.6 %all-gather.3.cloned.1.call-start = ((), (), s32[]{:S(2)}) async-start(), calls=%async_computation | async-start | bytes 3440640 | tf_op jit(solution)/shard_map/all_gather | solution.py:84
  9.2 5.1 copy-start.2
  10.4 4.6 collective-permute-start
  13.0 6.5 collective-permute-start.1
  45.7 222.9 %all-gather.5.cloned.1.call-start = ((), (), s32[]{:S(2)}) async-start(), calls=%async_computation.1 | async-start | bytes 6522880 | tf_op jit(solution)/shard_map/all_gather | solution.py:88
  283.9 248.0 %copy-start.1 = (f32[896]{0:T(1024)S(1)}, f32[896]{0:T(1024)}, u32[]{:S(2)}) copy-start(f32[896]{0:T(1024)} %param.10) | copy-start | bytes 10756
Sparse Core Ops, SparseCore 0:
  45.8 59.8 all-gather.2
  109.0 159.5 all-gather.4
where the time goes:
time: 1190 us
  blocking collectives  906 us (76%)
  waiting for transfers between devices  227 us (19%)
  matrix products  18.3 us (2%)
  between operations  15.9 us (1%)
  local copies, waits for them, and re-layouts  13.2 us (1%)
    psum x1, blocking collectives, local(): lax.psum(local_penalty, ('frames', 'mp'))  649 us
    psum x1, blocking collectives, local(): lax.psum(feature_sums, ('frames', 'dp'))  248 us
    all_gather x1, waiting for transfers between devices, local(): lax.all_gather(out_weight, 'frames', axis=0, tiled=True)  163 us
    all_gather x1, waiting for transfers between devices, local(): gathered = lax.all_gather(attended, 'mp', axis=3, tiled=True)  59.2 us
  transfers between devices with their start and end apart: 4, of which 3 were waited for; matrix products, arithmetic and copies ran while one was open for 0% of the time, Pallas kernels for 0%

commit v1 on v0

--- a/solution.py
+++ b/solution.py
@@ -96,7 +96,7 @@
     difference = (normed[1] - normed[0]) * own_live
     feature_sums = jnp.sum(difference * difference, axis=(0, 1))
     local_penalty = jnp.sum(feature_sums * norm_gain * norm_gain).reshape(1)
-    penalty = lax.psum(local_penalty, ("frames", "mp")) / (
+    penalty = lax.psum(lax.psum(local_penalty, "frames"), "mp") / (
         sigma_noise * sigma_noise * token_total * model_width
     )
     gain_grad = (

time: 1190 us -> 683 us (0.57)
  blocking collectives: 906 us -> 396 us
    psum x1 -> x2, blocking collectives: 649 us -> 140 us  [the longest x1 129 us: local(): lax.psum(local_penalty, 'frames')]
where the time goes in v1:
time: 683 us
  blocking collectives  396 us (58%)
  waiting for transfers between devices  227 us (33%)
  matrix products  18.3 us (3%)
  between operations  15.9 us (2%)
  local copies, waits for them, and re-layouts  13.2 us (2%)
  other arithmetic  7.59 us (1%)
    psum x1, blocking collectives, local(): lax.psum(feature_sums, ('frames', 'dp'))  248 us
    all_gather x1, waiting for transfers between devices, local(): lax.all_gather(out_weight, 'frames', axis=0, tiled=True)  163 us
    psum x1, blocking collectives, local(): lax.psum(local_penalty, 'frames')  129 us
    all_gather x1, waiting for transfers between devices, local(): gathered = lax.all_gather(attended, 'mp', axis=3, tiled=True)  59.2 us
  transfers between devices with their start and end apart: 4, of which 3 were waited for; matrix products, arithmetic and copies ran while one was open for 0% of the time, Pallas kernels for 0%

profile of v1, /device:TPU:2, one launch (start us, length us, event | category | flops | bytes accessed | tf_op | source)
XLA Modules:
  0.0 682.7 jit_solution(3711684249170791057)
XLA Ops:
  7.2 0.0 copy-start
  7.2 0.0 all-gather.3.cloned.1.call-start
  7.2 1.9 add_convert_fusion
  9.1 0.0 copy-done
  9.2 0.0 copy-start.2
  9.2 1.2 fusion.25
  10.4 2.6 collective-permute-start
  13.0 1.3 collective-permute-start.1
  14.3 0.1 pad_dynamic-slice_fusion
  14.4 0.1 lt.41
  14.5 0.1 lt.42
  14.5 0.1 lt.43
  14.6 0.1 lt.38
  14.7 0.1 pad_maximum_fusion.1
  14.8 0.1 fusion.23
  15.0 0.0 collective-permute-done
  15.0 4.5 collective-permute-done.1
  19.5 1.7 pad_maximum_fusion
  21.2 0.3 copy.13
  21.5 1.3 slice_bitcast_fusion
  22.8 22.9 %while.10 = (s32[]{:T(128)}, bf16[4,96,896]{2,1,0:T(8,128)(2,1)}, bf16[4,192,896]{2,1,0:T(8,128)(2,1)}, pred[4,192]{1,0:T(4,128)(4,1)S(1)}, bf16[4,96,896]{2,1,0...) while((s32[]{:T(128)}, bf16[4,96,896]{2,1,0:T(8,128)(2,1)}, bf16[4,192,896]{2,1,0:T(8,128)(2,1)}, ...), condition=%wide.region_3.4_spmd, body=%wide.region_0.3_spmd.sunk | while | flops 67049856 | bytes 5857369 | solution.py:59
  22.8 1.0 constant_dynamic-slice_fusion.5
  23.8 0.4 reshape.106
  24.3 0.2 reshape.107
  24.5 1.5 fusion.45
  26.0 0.4 reshape.108
  26.4 1.4 fusion.46
  27.8 0.7 bitcast_dynamic-update-slice_fusion.2
  28.5 1.0 constant_dynamic-slice_fusion.5
  29.5 0.4 reshape.106
  30.0 0.2 reshape.107
  30.2 1.5 fusion.45
  31.7 0.4 reshape.108
  32.1 1.4 fusion.46
  33.5 0.7 bitcast_dynamic-update-slice_fusion.2
  34.2 1.0 constant_dynamic-slice_fusion.5
  35.3 0.4 reshape.106
  35.7 0.2 reshape.107
  36.0 1.5 fusion.45
  37.5 0.4 reshape.108
  37.9 1.4 fusion.46
  39.3 0.7 bitcast_dynamic-update-slice_fusion.2
  40.0 1.0 constant_dynamic-slice_fusion.5
  41.0 0.4 reshape.106
  41.5 0.2 reshape.107
  41.7 1.5 fusion.45
  43.2 0.4 reshape.108
  43.6 1.4 fusion.46
  45.0 0.7 bitcast_dynamic-update-slice_fusion.2
  45.7 0.0 all-gather.3.cloned.1.call-update
  45.7 0.0 all-gather.5.cloned.1.call-start
  45.8 0.7 all-gather.5.cloned.1.call-update
  46.5 0.1 iota_compare_fusion
  46.5 59.2 %all-gather.3.cloned.1.call-done = bf16[2,2,96,3584]{3,2,1,0:T(8,128)(2,1)} async-done(((bf16[2,2,96,896]{3,2,1,0:T(8,128)(2,1)}), bf16[2,2,96,3584]{3,2,1,0:T(8,128)(2,1)}) %all-gather.3.cloned.1.call-update) | async-done | bytes 2752528 | tf_op jit(solution)/shard_map/all_gather | solution.py:84
  105.8 162.8 %all-gather.5.cloned.1.call-done = bf16[3584,896]{1,0:T(8,128)(2,1)} async-done(((bf16[56,896]{1,0:T(8,128)(2,1)}), bf16[3584,896]{1,0:T(8,128)(2,1)}) %all-gather.5.cloned.1.call-update) | async-done | bytes 6422544 | tf_op jit(solution)/shard_map/all_gather | solution.py:88
  268.6 6.7 multiply_reduce_fusion
  275.3 8.6 %psum.28 = f32[2,2,96]{2,1,0:T(2,128)S(1)} all-reduce(f32[2,2,96]{2,1,0:T(2,128)S(1)} %get-tuple-element.58), channel_id=1, replica_groups=mesh['frames'=64,'mp'=4,'dp'=2] {'mp'}, use_global_device_ids=true, to_apply=%region_5.6 | all-reduce | flops 384 | bytes 3072 | tf_op jit(solution)/shard_map/psum | solution.py:92
  283.9 0.2 broadcast_multiply_fusion
  284.1 0.2 fusion.29
  284.3 247.6 %psum.31 = f32[896]{0:T(1024)S(1)} all-reduce(f32[896]{0:T(1024)S(1)} %fusion.29), channel_id=1, replica_groups=mesh['frames'=64,'mp'=4,'dp'=2] {'frames','dp'}, use_global_device_ids=true, to_apply=%region_10.11 | all-reduce | flops 896 | bytes 7168 | tf_op jit(solution)/shard_map/psum | solution.py:104
  532.0 1.2 multiply_multiply_fusion.1
  533.2 129.4 %psum.29 = f32[1]{0:T(128)} all-reduce(f32[1]{0:T(128)} %bitcast.11), channel_id=1, replica_groups=mesh['frames'=64,'mp'=4,'dp'=2] {'frames'}, use_global_device_ids=true, to_apply=%region_8.9 | all-reduce | flops 1 | bytes 8 | tf_op jit(solution)/shard_map/psum | solution.py:99
  662.5 0.8 multiply_convert_fusion
  663.4 10.7 %psum.30 = f32[1]{0:T(128)} all-reduce(f32[1]{0:T(128)} %psum.29), channel_id=1, replica_groups=mesh['frames'=64,'mp'=4,'dp'=2] {'mp'}, use_global_device_ids=true, to_apply=%region_9.10 | all-reduce | flops 1 | bytes 8 | tf_op jit(solution)/shard_map/psum | solution.py:99
  (22 shorter events, 0.3 us)
Async XLA Ops:
  7.2 2.0 copy-start
  7.2 98.6 %all-gather.3.cloned.1.call-start = ((), (), s32[]{:S(2)}) async-start(), calls=%async_computation | async-start | bytes 3440640 | tf_op jit(solution)/shard_map/all_gather | solution.py:84
  9.2 5.1 copy-start.2
  10.4 4.6 collective-permute-start
  13.0 6.5 collective-permute-start.1
  45.7 222.9 %all-gather.5.cloned.1.call-start = ((), (), s32[]{:S(2)}) async-start(), calls=%async_computation.1 | async-start | bytes 6522880 | tf_op jit(solution)/shard_map/all_gather | solution.py:88
  283.9 248.0 %copy-start.1 = (f32[896]{0:T(1024)S(1)}, f32[896]{0:T(1024)}, u32[]{:S(2)}) copy-start(f32[896]{0:T(1024)} %param.10) | copy-start | bytes 10756
Sparse Core Ops, SparseCore 0:
  45.8 59.8 all-gather.2
  109.0 159.5 all-gather.4
